TPU v7x, 32 devices: a whole 2x2x4 slice. The times are simulated.
32 devices in a mesh: grp: 2 (over x), ep: 4 (over y, core), dp: 4 (over z).
Axes of the slice: x: 2, y: 2, z: 4, core: 2. Of those that a mesh axis runs over, the one named last changes fastest.
Arguments:
- hidden_states: bfloat16 [512, 7168], P(('grp', 'ep'), 'dp'), parts along dimension 0, may hold values from -27 to 27
- input_gain: float32 [7168], P('dp'), may hold values from 0.25 to 1.75
- expert_ids: int32 [512, 2], P(('grp', 'ep')), parts along dimension 0, may hold values from 0 to 3, all different within a row; in each aligned block of 64 rows (0 to 63, 64 to 127, ...) at most 64 rows name the same one
- route_scores: float32 [512, 2], P(('grp', 'ep')), parts along dimension 0, may hold values from 0.05 to 1
- w_gate: bfloat16 [4, 7168, 2048], P('ep', None, 'dp'), may hold values from -0.0625 to 0.0625
- w_up: bfloat16 [4, 7168, 2048], P('ep', None, 'dp'), may hold values from -0.0625 to 0.0625
- w_down: bfloat16 [4, 2048, 7168], P('ep', 'dp'), may hold values from -0.1875 to 0.1875
- latent_gain: float32 [7168], P('dp'), may hold values from 0.25 to 1.75
- w_latent: bfloat16 [7168, 576], P('dp'), may hold values from -0.0625 to 0.0625
- kv_gain: float32 [512], replicated, may hold values from 0.25 to 1.75
- seq_lengths: int32 [8, 4], P(('grp', 'ep')), parts along dimension 0, may hold values from 1 to 32, 64 in all within a row
- seq_owners: int32 [8, 4], P(('grp', 'ep')), parts along dimension 0, may hold values from 0 to 3
Outputs:
- mixed_states: bfloat16 [512, 7168], P(('grp', 'ep'), 'dp'), parts along dimension 0
- latent_cache: bfloat16 [8, 4, 64, 576], P(('grp', 'ep'), 'dp'), parts along dimension 0
There are 2 independent parts, one for each index of `grp`. A program takes and returns all parts, laid end to end along the dimension named above; an argument that names none is the same for every part. Nothing has to cross between parts.
Inputs may be any that keep to these rules, and one draw needn't show every extreme that they name: `expert_ids`: each row names 2 different experts; among the 64 rows of one ep block no expert is named more than 64 times, and some block reaches 64. `seq_lengths`: each row sums to 64 and holds one length of exactly 32.
All inputs are finite; a program needn't handle non-finite values.
Results may differ from a plain program's by a relative error of at most 0.015.
Values may be sent and summed in bfloat16 or wider, within the bound.
A program may use at most 128 MiB of HBM per device.

v0:
```python
import math

import jax
import jax.numpy as jnp
from jax import lax
from jax.sharding import PartitionSpec as P

EPSILON = 1e-06
ROUTE_SCALE = 2.5


def slot_table(block_ids, expert_count):
    flat_ids = block_ids.reshape(-1)
    one_hot = (flat_ids[:, None] == jnp.arange(expert_count, dtype=jnp.int32)[None, :]).astype(
        jnp.int32
    )
    earlier = jnp.cumsum(one_hot, axis=0) - one_hot
    return (flat_ids, jnp.sum(earlier * one_hot, axis=1))


def sequence_info(token_index, seq_lengths, seq_owners):
    seq_ends = jnp.cumsum(seq_lengths)
    seq_number = jnp.sum((token_index[:, None] >= seq_ends[None, :]).astype(jnp.int32), axis=1)
    member = (
        seq_number[:, None] == jnp.arange(seq_lengths.shape[0], dtype=jnp.int32)[None, :]
    ).astype(jnp.int32)
    seq_starts = seq_ends - seq_lengths
    positions = token_index - jnp.sum(member * seq_starts[None, :], axis=1)
    owner_of = jnp.sum(member * seq_owners[None, :], axis=1)
    return (positions, owner_of)


def rope_rotate(rope_keys, positions, rope_width):
    half_width = rope_width // 2
    frequency = jnp.exp(
        jnp.arange(half_width, dtype=jnp.float32) * (-2.0 * math.log(10000.0) / rope_width)
    )
    angles = positions.astype(jnp.float32)[:, None] * frequency[None, :]
    cosine = jnp.cos(angles)
    sine_part = jnp.sin(angles)
    first_half = rope_keys[:, :half_width]
    second_half = rope_keys[:, half_width:]
    return jnp.concatenate(
        [
            first_half * cosine - second_half * sine_part,
            second_half * cosine + first_half * sine_part,
        ],
        axis=1,
    )


def finish_latent(latent_sum, positions, kv_gain):
    kv_width = kv_gain.shape[0]
    compressed = latent_sum[:, :kv_width]
    mean_square = jnp.mean(compressed * compressed, axis=1, keepdims=True)
    normed_kv = compressed * lax.rsqrt(mean_square + EPSILON) * kv_gain[None, :]
    rotated = rope_rotate(latent_sum[:, kv_width:], positions, latent_sum.shape[1] - kv_width)
    return jnp.concatenate([normed_kv, rotated], axis=1).astype(jnp.bfloat16)


def owner_rows(finished, owner_of, owner_index):
    owned_mask = (owner_of == owner_index).astype(jnp.int32)
    row_rank = jnp.cumsum(owned_mask) - owned_mask
    picker = (
        (row_rank[None, :] == jnp.arange(finished.shape[0], dtype=jnp.int32)[:, None])
        & (owned_mask[None, :] == 1)
    ).astype(jnp.bfloat16)
    return jnp.dot(picker, finished, preferred_element_type=jnp.float32).astype(jnp.bfloat16)


def expert_hidden(gate_sum, up_sum):
    return (jax.nn.silu(gate_sum) * up_sum).astype(jnp.bfloat16)


def on_device(
    hidden_states,
    input_gain,
    expert_ids,
    route_scores,
    w_gate,
    w_up,
    w_down,
    latent_gain,
    w_latent,
    kv_gain,
    seq_lengths,
    seq_owners,
):
    tok_block, feat_shard = hidden_states.shape
    top_count = expert_ids.shape[1]
    ep_count = lax.axis_size("ep")
    dp_count = lax.axis_size("dp")
    model_width = feat_shard * dp_count
    capacity = 2 * tok_block * top_count // ep_count
    gate_matrix = w_gate[0]
    up_matrix = w_up[0]
    down_matrix = w_down[0]
    states = hidden_states.astype(jnp.float32)
    square_sum = lax.psum(jnp.sum(states * states, axis=1), "dp")
    normed = (
        states * lax.rsqrt(square_sum / model_width + EPSILON)[:, None] * input_gain[None, :]
    ).astype(jnp.bfloat16)
    flat_ids, slot_index = slot_table(expert_ids, ep_count)
    row_slot = slot_index * ep_count + flat_ids
    token_of = jnp.repeat(jnp.arange(tok_block, dtype=jnp.int32), top_count)
    send_rows = (
        jnp.zeros((capacity * ep_count, feat_shard), jnp.bfloat16)
        .at[row_slot]
        .set(normed[token_of])
    )
    send_rows = send_rows.reshape(capacity, ep_count, feat_shard)
    arrived = lax.all_to_all(send_rows, "ep", split_axis=1, concat_axis=1, tiled=True)
    item_count = arrived.shape[0]
    row_count = item_count * ep_count
    feature_piece = lax.all_gather(arrived, "dp", axis=2, tiled=True)
    piece_width = feature_piece.shape[2]
    piece_rows = feature_piece.reshape(row_count, piece_width)
    gate_sum = jnp.dot(piece_rows, gate_matrix, preferred_element_type=jnp.float32)
    up_sum = jnp.dot(piece_rows, up_matrix, preferred_element_type=jnp.float32)
    hidden_units = expert_hidden(gate_sum, up_sum)
    partial_value = jnp.dot(hidden_units, down_matrix, preferred_element_type=jnp.float32)
    shard_sum = lax.psum_scatter(
        partial_value.astype(jnp.bfloat16), "dp", scatter_dimension=1, tiled=True
    )
    shard_out = shard_sum.reshape(item_count, ep_count, feat_shard)
    expert_out = lax.all_to_all(shard_out, "ep", split_axis=1, concat_axis=1, tiled=True)
    picked = expert_out.reshape(capacity * ep_count, feat_shard)[row_slot]
    picked = picked.astype(jnp.float32).reshape(tok_block, top_count, feat_shard)
    route_weights = ROUTE_SCALE * route_scores / jnp.sum(route_scores, axis=1, keepdims=True)
    mixed_states = (states + jnp.sum(route_weights[:, :, None] * picked, axis=1)).astype(
        jnp.bfloat16
    )
    layer_out = mixed_states.astype(jnp.float32)
    out_square = lax.psum(jnp.sum(layer_out * layer_out, axis=1), "dp")
    normed_out = (
        layer_out * lax.rsqrt(out_square / model_width + EPSILON)[:, None] * latent_gain[None, :]
    ).astype(jnp.bfloat16)
    latent_part = jnp.dot(normed_out, w_latent, preferred_element_type=jnp.float32)
    token_index = jnp.arange(tok_block, dtype=jnp.int32)
    positions, owner_of = sequence_info(token_index, seq_lengths[0], seq_owners[0])
    latent_total = lax.psum(latent_part.astype(jnp.bfloat16), "dp").astype(jnp.float32)
    finished = finish_latent(latent_total, positions, kv_gain)
    cache_rows = owner_rows(finished, owner_of, lax.axis_index("dp"))
    return (mixed_states, cache_rows[None, None])


def solution(mesh):
    return jax.shard_map(
        on_device,
        mesh=mesh,
        in_specs=(
            P(("grp", "ep"), "dp"),
            P("dp"),
            P(("grp", "ep"), None),
            P(("grp", "ep"), None),
            P("ep", None, "dp"),
            P("ep", None, "dp"),
            P("ep", "dp", None),
            P("dp"),
            P("dp", None),
            P(),
            P(("grp", "ep"), None),
            P(("grp", "ep"), None),
        ),
        out_specs=(P(("grp", "ep"), "dp"), P(("grp", "ep"), "dp", None, None)),
        check_vma=False,
    )
```

profile of v0, /device:TPU:0, one launch (start us, length us, event | category | flops | bytes accessed | tf_op | source)
XLA Modules:
  0.0 295.1 jit_solution(15307027982889255500)
XLA Ops:
  7.2 0.0 copy-start
  7.2 0.0 all-gather.2.cloned.1.call-start
  7.2 0.9 copy.45
  8.1 0.1 eq.75
  8.3 0.1 reshape.166
  8.4 0.1 fusion.38
  8.5 0.2 reduce_window_sum.25
  8.7 0.2 select_reduce_fusion
  8.9 1.1 fusion.22
  9.9 13.5 %psum.21 = f32[64]{0:T(128)S(1)} all-reduce(f32[64]{0:T(128)S(1)} %fusion.22), channel_id=1, replica_groups=mesh['grp'=2,'ep'=4,'dp'=4] {'dp'}, use_global_device_ids=true, to_apply=%region_4.5 | all-reduce | flops 64 | bytes 512 | tf_op jit(solution)/shard_map/psum | solution.py:99
  23.4 0.1 reshape.167
  23.6 1.1 fusion.24
  24.7 3.0 %scatter_custom_fusion = bf16[256,1792]{1,0:T(8,128)(2,1)S(1)} fusion(s32[128]{0:T(128)S(1)} %fusion.51, bf16[64,1792]{1,0:T(8,128)(2,1)S(1)} %fusion.24, s32[1024]{0:T(1024)S(1)} %pad_clamp_fusion.1, bf16[]{:T(256)} %constant.16.clone.1), kind=kCustom, calls=%fused_computation.32 | custom fusion | bytes 917506 | tf_op jit(solution)/shard_map/scatter | solution.py:109
  27.7 1.1 reshape.168
  28.9 1.3 copy.47
  30.1 16.2 %all_to_all.10 = bf16[64,4,1792]{2,0,1:T(8,128)(2,1)} all-to-all(bf16[64,4,1792]{2,0,1:T(8,128)(2,1)S(1)} %copy.47), channel_id=1, replica_groups=mesh['grp'=2,'ep'=4,'dp'=4] {'ep'}, dimensions={1} | all-to-all | bytes 1835008 | tf_op jit(solution)/shard_map/all_to_all | solution.py:112
  46.3 0.0 all-gather.2.cloned.1.call-update
  46.3 0.2 reduce-scatter.2.cloned.1.call-start
  46.6 69.3 %all-gather.2.cloned.1.call-done = bf16[64,4,7168]{2,0,1:T(8,128)(2,1)} async-done(((bf16[64,4,1792]{2,0,1:T(8,128)(2,1)}), bf16[64,4,7168]{2,0,1:T(8,128)(2,1)}) %all-gather.2.cloned.1.call-update) | async-done | bytes 3670032 | tf_op jit(solution)/shard_map/all_gather | solution.py:115
  115.9 6.7 %copy.48 = bf16[64,4,7168]{2,1,0:T(4,128)(2,1)} copy(bf16[64,4,7168]{2,0,1:T(8,128)(2,1)} %all-gather.2.cloned.1.call-done) | data formatting | bytes 7340032 | tf_op jit(solution)/shard_map/all_gather | solution.py:115
  122.6 6.7 %reshape.169 = bf16[256,7168]{1,0:T(8,128)(2,1)} reshape(bf16[64,4,7168]{2,1,0:T(4,128)(2,1)} %copy.48) | data formatting | bytes 7340032 | tf_op jit(solution)/shard_map/reshape | solution.py:117
  129.3 6.2 %fusion.3 = f32[256,512]{1,0:T(8,128)S(1)} fusion(bf16[256,7168]{1,0:T(8,128)(2,1)} %reshape.169, bf16[1,7168,512]{2,1,0:T(8,128)(2,1)} %param.16), kind=kOutput, calls=%fused_computation.7 | convolution fusion | flops 1879048192 | bytes 11534336 | tf_op jit(solution)/shard_map/dot_general | solution.py:118
  135.6 12.1 %convolution_convert_fusion = bf16[256,7168]{1,0:T(8,128)(2,1)} fusion(bf16[1,512,7168]{2,1,0:T(8,128)(2,1)} %param.18, bf16[256,7168]{1,0:T(8,128)(2,1)} %reshape.169, bf16[1,7168,512]{2,1,0:T(8,128)(2,1)} %param.17, f32[256,512]{1,0:T(8,128)S(1)} %fusion.3), kind=kOutput, calls=%fused_computation.3 | convolution fusion | flops 3760717824 | bytes 22544384 | tf_op jit(solution)/shard_map/dot_general | solution.py:121
  147.7 0.0 copy-start.7
  147.7 0.0 reduce-scatter.2.cloned.1.call-update
  147.7 0.0 copy-start.6
  147.7 0.6 copy-done.7
  148.3 0.2 reduce-window.13
  148.5 0.0 copy-done.4
  148.6 66.3 %reduce-scatter.2.cloned.1.call-done = bf16[256,1792]{1,0:T(8,128)(2,1)} async-done(((bf16[256,7168]{1,0:T(8,128)(2,1)}), bf16[256,1792]{1,0:T(8,128)(2,1)}) %reduce-scatter.2.cloned.1.call-update) | async-done | bytes 917520 | tf_op jit(solution)/shard_map/reduce_scatter | solution.py:122
  214.9 1.8 reshape.170
  216.7 1.0 copy.49
  217.7 3.5 %all-to-all-start.1 = ((bf16[64,4,1792]{2,0,1:T(8,128)(2,1)}), bf16[64,4,1792]{2,0,1:T(8,128)(2,1)S(1)}, u32[]{:S(2)}, u32[]{:S(2)}) async-start(bf16[64,4,1792]{2,0,1:T(8,128)(2,1)} %copy.49), calls=%async_computation.2 | async-start | bytes 1835008 | tf_op jit(solution)/shard_map/all_to_all | solution.py:126
  221.2 0.3 all-reduce.2.cloned.1.call-start
  221.5 0.1 convert_reduce_fusion
  221.6 0.1 copy.44
  221.7 0.0 copy-done.6
  221.7 0.1 select_reduce_fusion.2
  221.8 0.1 copy.51
  221.9 0.1 reduce-window.14
  222.0 0.1 reduce
  222.1 12.1 %all-to-all-done.1 = bf16[64,4,1792]{2,0,1:T(8,128)(2,1)S(1)} async-done(((bf16[64,4,1792]{2,0,1:T(8,128)(2,1)}), bf16[64,4,1792]{2,0,1:T(8,128)(2,1)S(1)}, u32[]{:S(2)}, u32[]{:S(2)}) %all-to-all-start.1) | async-done | bytes 917536 | tf_op jit(solution)/shard_map/all_to_all | solution.py:126
  234.2 1.6 copy.50
  235.9 1.6 reshape.171
  237.5 0.0 copy-start.1
  237.5 0.0 copy-start.3
  237.6 1.7 gather_fusion
  239.3 1.5 reshape.175
  240.7 1.3 multiply_reduce_fusion
  242.0 0.0 copy-done.1
  242.0 0.2 fusion.19
  242.2 10.8 %psum.22 = f32[64]{0:T(128)S(1)} all-reduce(f32[64]{0:T(128)S(1)} %get-tuple-element.4), channel_id=1, replica_groups=mesh['grp'=2,'ep'=4,'dp'=4] {'dp'}, use_global_device_ids=true, to_apply=%region_13.14 | all-reduce | flops 64 | bytes 512 | tf_op jit(solution)/shard_map/psum | solution.py:134
  253.0 0.0 copy-done
  253.0 0.0 copy-done.3
  253.0 1.4 convolution_convert_fusion.1
  254.4 0.0 all-reduce.2.cloned.1.call-update
  254.5 31.9 %all-reduce.2.cloned.1.call-done = bf16[64,576]{0,1:T(8,128)(2,1)} async-done(((bf16[64,576]{0,1:T(8,128)(2,1)}), bf16[64,576]{0,1:T(8,128)(2,1)}) %all-reduce.2.cloned.1.call-update) | async-done | bytes 73744 | tf_op jit(solution)/shard_map/psum | solution.py:141
  286.4 0.9 convert_element_type.92
  287.3 0.1 multiply_reduce_fusion.1
  287.4 0.0 copy-done.5
  287.4 0.1 multiply_convert_fusion
  287.6 0.1 fusion.46
  287.7 0.8 fusion.11
  288.6 0.0 copy-done.2
  (17 shorter events, 0.1 us)
Async XLA Ops:
  7.2 245.9 %copy-start = (bf16[1792,576]{0,1:T(8,128)(2,1)S(1)}, bf16[1792,576]{0,1:T(8,128)(2,1)}, u32[]{:S(2)}) copy-start(bf16[1792,576]{0,1:T(8,128)(2,1)} %param.20) | copy-start | bytes 6193156
  7.2 108.7 %all-gather.2.cloned.1.call-start = ((), (), s32[]{:S(2)}) async-start(), calls=%async_computation.3 | async-start | bytes 4587520 | tf_op jit(solution)/shard_map/all_gather | solution.py:115
  46.3 168.5 %reduce-scatter.2.cloned.1.call-start = ((), (), s32[]{:S(2)}) async-start(), calls=%async_computation.4 | async-start | bytes 4587520 | tf_op jit(solution)/shard_map/reduce_scatter | solution.py:122
  147.7 0.7 copy-start.7
  147.7 0.8 copy-start.4
  147.7 74.0 %copy-start.6 = (s32[1,4]{1,0:T(1,128)S(1)}, s32[1,4]{1,0:T(1,128)}, u32[]{:S(2)}) copy-start(s32[1,4]{1,0:T(1,128)} %param.23) | copy-start | bytes 52
  217.7 16.5 %all-to-all-start.1 = ((bf16[64,4,1792]{2,0,1:T(8,128)(2,1)}), bf16[64,4,1792]{2,0,1:T(8,128)(2,1)S(1)}, u32[]{:S(2)}, u32[]{:S(2)}) async-start(bf16[64,4,1792]{2,0,1:T(8,128)(2,1)} %copy.49), calls=%async_computation.2 | async-start | bytes 1835008 | tf_op jit(solution)/shard_map/all_to_all | solution.py:126
  221.2 65.2 %all-reduce.2.cloned.1.call-start = ((), (), s32[]{:S(2)}) async-start(), calls=%async_computation.5 | async-start | bytes 294912 | tf_op jit(solution)/shard_map/psum | solution.py:141
  237.5 4.5 %copy-start.1 = (bf16[64,1792]{1,0:T(8,128)(2,1)S(1)}, bf16[64,1792]{1,0:T(8,128)(2,1)}, u32[]{:S(2)}) copy-start(bf16[64,1792]{1,0:T(8,128)(2,1)} %param.12) | copy-start | bytes 688132
  237.5 15.5 %copy-start.3 = (f32[1792]{0:T(1024)S(1)}, f32[1792]{0:T(1024)}, u32[]{:S(2)}) copy-start(f32[1792]{0:T(1024)} %param.19) | copy-start | bytes 21508
  239.3 48.2 %copy-start.5 = (f32[512]{0:T(512)S(1)}, f32[512]{0:T(512)}, u32[]{:S(2)}) copy-start(f32[512]{0:T(512)} %param.21) | copy-start | bytes 6148
  242.2 46.4 %copy-start.2 = (bf16[64,1792]{1,0:T(8,128)(2,1)}, bf16[64,1792]{1,0:T(8,128)(2,1)S(1)}, u32[]{:S(2)}) copy-start(bf16[64,1792]{1,0:T(8,128)(2,1)S(1)} %get-tuple-element.5) | copy-start | bytes 688132
Sparse Core Ops, SparseCore 0:
  46.5 69.3 all-gather.1
  147.8 67.0 reduce-scatter.1
  254.6 31.7 all-reduce.1
where the time goes:
time: 296 us; the launch traced here: 295 us
  waiting for transfers between devices  180 us (61%)
  blocking collectives  40.5 us (14%)
  local copies, waits for them, and re-layouts  30.3 us (10%)
  matrix products  20.6 us (7%)
  between operations  14 us (5%)
  other arithmetic  5.99 us (2%)
  starting transfers between devices  4.03 us (1%)
    all_gather x1, waiting for transfers between devices, on_device(): feature_piece = lax.all_gather(arrived, 'dp', axis=2, tiled=True)  69.3 us
    reduce_scatter x1, waiting for transfers between devices, on_device(): lax.psum_scatter(partial_value.astype(jnp.bfloat16), 'dp', scatter_dimens...  66.3 us
    psum x1, waiting for transfers between devices, on_device(): lax.psum(latent_part.astype(jnp.bfloat16), 'dp').astype(jnp.float32)  31.9 us
    all_to_all x1, blocking collectives, on_device(): lax.all_to_all(send_rows, 'ep', split_axis=1, concat_axis=1, tiled=True)  16.2 us
    psum x1, blocking collectives, on_device(): square_sum = lax.psum(jnp.sum(states * states, axis=1), 'dp')  13.5 us
    all_to_all x1, waiting for transfers between devices, on_device(): lax.all_to_all(shard_out, 'ep', split_axis=1, concat_axis=1, tiled=True)  12.1 us
    dot_general x1, matrix products, on_device(): jnp.dot(hidden_units, down_matrix, preferred_element_type=jnp.float32)  12.1 us
    psum x1, blocking collectives, on_device(): out_square = lax.psum(jnp.sum(layer_out * layer_out, axis=1), 'dp')  10.8 us
  transfers between devices with their start and end apart: 4, of which 4 were waited for; matrix products, arithmetic and copies ran while one was open for 0% of the time, Pallas kernels for 0%

commit v1 on v0

v1 whole, which is shorter than its diff:
```python
import functools
import math

import jax
import jax.numpy as jnp
from jax import lax
from jax.experimental import pallas as pl
from jax.experimental.pallas import tpu as pltpu
from jax.sharding import PartitionSpec as P

EPSILON = 1e-06
ROUTE_SCALE = 2.5
LANES = 128
F32 = jnp.float32
BF16 = jnp.bfloat16


def flipped(index, k, count):
    out = index
    bit = 1
    while bit < count:
        out = out + bit * ((k // bit) % 2) * (1 - 2 * ((index // bit) % 2))
        bit *= 2
    return out


def loop(lower, upper, body):
    def step(i, carry):
        body(i)
        return carry

    lax.fori_loop(lower, upper, step, 0)


def split_f32(value):
    high = value.astype(BF16).astype(F32)
    return high, value - high


def kernel(
    n_ep,
    n_dp,
    states_ref,
    gain_ref,
    ids_ref,
    scores_ref,
    wg_hbm,
    wu_hbm,
    wd_hbm,
    lgain_ref,
    wl_hbm,
    kvgain_ref,
    lengths_ref,
    owners_ref,
    mixed_ref,
    cache_ref,
    xbuf,
    wg,
    wu,
    wd,
    wl,
    acc_g,
    acc_u,
    hid,
    crecv,
    yrecv,
    zrecv,
    latbuf,
    latrecv,
    w_sem,
    g_recv,
    gz_send,
    gy_send,
    gc_send,
    rc_send,
    rc_recv,
    ry_send,
    ry_recv,
    rz_send,
    rz_recv,
    l_send,
    l_recv,
):
    tok, fs = states_ref.shape
    top = ids_ref.shape[1]
    rows = n_ep * tok
    width = fs * n_dp
    n_y = n_ep // 2
    seqs = lengths_ref.shape[1]
    kvl = kvgain_ref.shape[1]
    lat_width = wl.shape[1]
    me = lax.axis_index("ep")
    z = lax.axis_index("dp")
    y = me // 2
    c = me % 2
    peer = y * 2 + (1 - c)

    def rem(src, dst, send, recv, **where):
        return pltpu.make_async_remote_copy(
            src_ref=src,
            dst_ref=dst,
            send_sem=send,
            recv_sem=recv,
            device_id=where,
            device_id_type=pl.DeviceIdType.MESH,
        )

    weight_copies = [
        pltpu.make_async_copy(wg_hbm.at[0], wg, w_sem.at[0]),
        pltpu.make_async_copy(wu_hbm.at[0], wu, w_sem.at[1]),
        pltpu.make_async_copy(wd_hbm.at[0], wd, w_sem.at[2]),
        pltpu.make_async_copy(wl_hbm, wl, w_sem.at[3]),
    ]

    barrier = pltpu.get_barrier_semaphore()
    for k in range(1, n_dp):
        pl.semaphore_signal(
            barrier, inc=1, device_id={"dp": flipped(z, k, n_dp)},
            device_id_type=pl.DeviceIdType.MESH,
        )
    for k in range(1, n_y):
        pl.semaphore_signal(
            barrier, inc=1, device_id={"ep": ((y + k) % n_y) * 2 + c},
            device_id_type=pl.DeviceIdType.MESH,
        )
    pl.semaphore_signal(
        barrier, inc=1, device_id={"ep": peer}, device_id_type=pl.DeviceIdType.MESH
    )

    states = states_ref[...].astype(F32)
    xbuf[z, me, :, pl.ds(0, fs)] = (states * gain_ref[...]).astype(BF16)
    square = jnp.sum(states * states, axis=1, keepdims=True)
    scores = scores_ref[...]
    weights = ROUTE_SCALE * scores / jnp.sum(scores, axis=1, keepdims=True)
    lane = lax.broadcasted_iota(jnp.int32, (tok, LANES), 1)
    half = LANES // 2
    folded = lane % half
    extra = jnp.where(folded == n_ep, square, 0.0)
    for k in range(top):
        extra += jnp.where(folded == ids_ref[:, k : k + 1], weights[:, k : k + 1], 0.0)
    high, low = split_f32(extra)
    xbuf[z, me, :, pl.ds(fs, LANES)] = jnp.where(lane < half, high, low).astype(BF16)

    pl.semaphore_wait(barrier, n_dp - 1 + n_y - 1 + 1)

    def gather_z(k):
        to = flipped(z, k, n_dp)
        return rem(xbuf.at[z, me], xbuf.at[z, me], gz_send.at[k], g_recv.at[z, me], dp=to)

    def gather_y(s, j):
        to = ((y + j) % n_y) * 2 + c
        return rem(xbuf.at[s, me], xbuf.at[s, me], gy_send.at[s, j], g_recv.at[s, me], ep=to)

    def gather_c(s, yy):
        b = yy * 2 + c
        return rem(xbuf.at[s, b], xbuf.at[s, b], gc_send.at[s, yy], g_recv.at[s, b], ep=peer)

    def gather_wait(s, b):
        rem(xbuf.at[s, b], xbuf.at[s, b], g_recv.at[s, b], g_recv.at[s, b], ep=peer).wait_recv()

    loop(1, n_dp, lambda k: gather_z(k).start())

    acc_g[...] = jnp.zeros_like(acc_g)
    acc_u[...] = jnp.zeros_like(acc_u)

    def gather_step(i):
        @pl.when(i < n_dp)
        def _():
            s = flipped(z, i, n_dp)

            @pl.when(i > 0)
            def _():
                gather_wait(s, me)

            loop(1, n_y, lambda j: gather_y(s, j).start())
            gather_c(s, y).start()

        @pl.when(i == 0)
        def _():
            for copy in weight_copies:
                copy.start()

        @pl.when((i >= 1) & (i <= n_dp))
        def _():
            s = flipped(z, i - 1, n_dp)

            def forward(j):
                yy = (y + j) % n_y
                gather_wait(s, yy * 2 + c)
                gather_c(s, yy).start()

            loop(1, n_y, forward)

        @pl.when(i == 2)
        def _():
            weight_copies[0].wait()
            weight_copies[1].wait()

        @pl.when(i >= 2)
        def _():
            s = flipped(z, i - 2, n_dp)
            loop(0, n_y, lambda yy: gather_wait(s, yy * 2 + (1 - c)))
            slab = xbuf[s, :, :, pl.ds(0, fs)].reshape(rows, fs)
            depth = pl.ds(pl.multiple_of(s * fs, LANES), fs)
            acc_g[...] += jnp.dot(slab, wg[depth, :], preferred_element_type=F32)
            acc_u[...] += jnp.dot(slab, wu[depth, :], preferred_element_type=F32)

    loop(0, n_dp + 2, gather_step)

    side = jnp.zeros((rows, LANES), F32)
    wide_lane = lax.broadcasted_iota(jnp.int32, (rows, LANES), 1) % half
    for s in range(n_dp):
        part = xbuf[s, :, :, pl.ds(fs, LANES)].reshape(rows, LANES).astype(F32)
        if s == 0:
            route = jnp.sum(jnp.where(wide_lane == me, part, 0.0), axis=1, keepdims=True)
        side += part
    total = jnp.sum(jnp.where(wide_lane == n_ep, side, 0.0), axis=1, keepdims=True)
    scale = lax.rsqrt(total / width + EPSILON)
    gate = acc_g[...] * scale
    up = acc_u[...] * scale
    hid[...] = (route * (gate / (1.0 + jnp.exp(-gate)) * up)).astype(BF16)

    loop(1, n_dp, lambda k: gather_z(k).wait_send())

    def gather_drain(s):
        loop(1, n_y, lambda j: gather_y(s, j).wait_send())
        loop(0, n_y, lambda yy: gather_c(s, yy).wait_send())

    loop(0, n_dp, gather_drain)
    weight_copies[2].wait()

    def slot(s, b):
        return xbuf.at[s, b, :, pl.ds(0, fs)]

    def reduce_c(s, yy):
        return rem(
            slot(s, yy * 2 + (1 - c)), crecv.at[s, yy], rc_send.at[s, yy], rc_recv.at[s, yy],
            ep=peer,
        )

    def reduce_y(s, j):
        to = (y + j) % n_y
        return rem(
            slot(s, to * 2 + c), yrecv.at[s, j], ry_send.at[s, j], ry_recv.at[s, j],
            ep=to * 2 + c,
        )

    def reduce_z(k):
        to = flipped(z, k, n_dp)
        return rem(slot(to, me), zrecv.at[k], rz_send.at[k], rz_recv.at[k], dp=to)

    tile = 256 if fs % 256 == 0 else LANES

    def reduce_step(i):
        @pl.when(i < n_dp)
        def _():
            s = flipped(z, n_dp - 1 - i, n_dp)
            for n in range(fs // tile):
                cols = pl.ds(pl.multiple_of(s * fs + n * tile, LANES), tile)
                out = jnp.dot(hid[...], wd[:, cols], preferred_element_type=F32)
                xbuf[s, :, :, pl.ds(n * tile, tile)] = out.astype(BF16).reshape(n_ep, tok, tile)
            loop(1, n_y + 1, lambda j: reduce_c(s, (y + j) % n_y).start())

        @pl.when((i >= 1) & (i <= n_dp))
        def _():
            s = flipped(z, n_dp - i, n_dp)

            def add(j):
                yy = (y + j) % n_y
                b = yy * 2 + c
                reduce_c(s, yy).wait_recv()
                xbuf[s, b, :, pl.ds(0, fs)] = (
                    xbuf[s, b, :, pl.ds(0, fs)].astype(F32) + crecv[s, yy].astype(F32)
                ).astype(BF16)

                @pl.when(j < n_y)
                def _():
                    reduce_y(s, j).start()

            loop(1, n_y + 1, add)

        @pl.when(i >= 2)
        def _():
            k = n_dp + 1 - i
            s = flipped(z, k, n_dp)

            def add(j):
                reduce_y(s, j).wait_recv()
                xbuf[s, me, :, pl.ds(0, fs)] = (
                    xbuf[s, me, :, pl.ds(0, fs)].astype(F32) + yrecv[s, j].astype(F32)
                ).astype(BF16)

            loop(1, n_y, add)

            @pl.when(k > 0)
            def _():
                reduce_z(k).start()

    loop(0, n_dp + 2, reduce_step)

    routed = xbuf[z, me, :, pl.ds(0, fs)].astype(F32)
    for k in range(n_dp - 1, 0, -1):
        reduce_z(k).wait_recv()
        routed += zrecv[k].astype(F32)
    mixed = (states_ref[...].astype(F32) + routed).astype(BF16)
    mixed_ref[...] = mixed

    layer = mixed.astype(F32)
    gained = (layer * lgain_ref[...]).astype(BF16)
    out_square = jnp.sum(layer * layer, axis=1, keepdims=True)
    weight_copies[3].wait()
    pad_width = latbuf.shape[1]
    latbuf[:, pl.ds(0, lat_width)] = jnp.dot(
        gained, wl[...], preferred_element_type=F32
    ).astype(BF16)
    high, low = split_f32(out_square)
    spare = lax.broadcasted_iota(jnp.int32, (tok, pad_width - lat_width), 1)
    latbuf[:, pl.ds(lat_width, pad_width - lat_width)] = jnp.where(
        spare == 0, high, jnp.where(spare == 1, low, 0.0)
    ).astype(BF16)

    def latent(k):
        return rem(
            latbuf, latrecv.at[k], l_send.at[k], l_recv.at[k], dp=flipped(z, k, n_dp)
        )

    for k in range(1, n_dp):
        latent(k).start()

    rope = lat_width - kvl
    turn = rope // 2
    tail = pad_width - kvl
    token = lax.broadcasted_iota(jnp.int32, (tok, tail), 0)
    across = lax.broadcasted_iota(jnp.int32, (tok, tok), 1)
    begin = jnp.int32(0)
    position = token
    owner = jnp.zeros((tok, tok), jnp.int32)
    for j in range(seqs):
        end = begin + lengths_ref[0, j]
        position = jnp.where((token >= begin) & (token < end), token - begin, position)
        owner = jnp.where((across >= begin) & (across < end), owners_ref[0, j], owner)
        begin = end
    column = lax.broadcasted_iota(jnp.int32, (tok, tail), 1)
    frequency = jnp.exp((column % turn).astype(F32) * (-2.0 * math.log(10000.0) / rope))
    angle = position.astype(F32) * frequency
    cosine = jnp.cos(angle)
    sine = jnp.sin(angle)
    sine = jnp.where(column < turn, -sine, sine)
    down = lax.broadcasted_iota(jnp.int32, (tok, tok), 0)
    mine = (owner == z).astype(F32)
    rank = jnp.dot(mine, (down < across).astype(F32), preferred_element_type=F32)
    picker = jnp.where((rank == down.astype(F32)) & (owner == z), 1.0, 0.0).astype(BF16)

    summed = latbuf[...].astype(F32)
    for k in range(1, n_dp):
        latent(k).wait_recv()
        summed += latrecv[k].astype(F32)
    end_part = summed[:, kvl:]
    in_square = jnp.where(
        (column == rope) | (column == rope + 1), end_part, 0.0
    )
    out_scale = lax.rsqrt(jnp.sum(in_square, axis=1, keepdims=True) / width + EPSILON)
    compressed = summed[:, :kvl] * out_scale
    mean_square = jnp.mean(compressed * compressed, axis=1, keepdims=True)
    normed = compressed * lax.rsqrt(mean_square + EPSILON) * kvgain_ref[...]
    keys = end_part * out_scale
    swapped = jnp.where(
        column < turn, pltpu.roll(keys, tail - turn, 1), pltpu.roll(keys, turn, 1)
    )
    rotated = keys * cosine + swapped * sine
    cache_ref[0, 0, :, pl.ds(0, kvl)] = jnp.dot(
        picker, normed.astype(BF16), preferred_element_type=F32
    ).astype(BF16)
    picked = jnp.dot(picker, rotated.astype(BF16), preferred_element_type=F32).astype(BF16)
    cache_ref[0, 0, :, pl.ds(kvl, rope)] = picked[:, :rope]

    for k in range(1, n_dp):
        latent(k).wait_send()
        reduce_z(k).wait_send()

    def reduce_drain(s):
        loop(1, n_y, lambda j: reduce_y(s, j).wait_send())
        loop(0, n_y, lambda yy: reduce_c(s, yy).wait_send())

    loop(0, n_dp, reduce_drain)


def on_device(
    hidden_states,
    input_gain,
    expert_ids,
    route_scores,
    w_gate,
    w_up,
    w_down,
    latent_gain,
    w_latent,
    kv_gain,
    seq_lengths,
    seq_owners,
):
    tok, fs = hidden_states.shape
    n_ep = lax.axis_size("ep")
    n_dp = lax.axis_size("dp")
    n_y = n_ep // 2
    rows = n_ep * tok
    width, units = w_gate.shape[1:]
    lat_width = w_latent.shape[1]
    kvl = kv_gain.shape[0]
    pad_width = kvl + LANES
    vmem = pl.BlockSpec(memory_space=pltpu.VMEM)
    hbm = pl.BlockSpec(memory_space=pl.ANY)
    smem = pl.BlockSpec(memory_space=pltpu.SMEM)
    dma = pltpu.SemaphoreType.DMA
    return pl.pallas_call(
        functools.partial(kernel, n_ep, n_dp),
        out_shape=(
            jax.ShapeDtypeStruct((tok, fs), BF16),
            jax.ShapeDtypeStruct((1, 1, tok, lat_width), BF16),
        ),
        in_specs=[vmem, vmem, vmem, vmem, hbm, hbm, hbm, vmem, hbm, vmem, smem, smem],
        out_specs=(vmem, vmem),
        scratch_shapes=[
            pltpu.VMEM((n_dp, n_ep, tok, fs + LANES), BF16),
            pltpu.VMEM((width, units), BF16),
            pltpu.VMEM((width, units), BF16),
            pltpu.VMEM((units, width), BF16),
            pltpu.VMEM((fs, lat_width), BF16),
            pltpu.VMEM((rows, units), F32),
            pltpu.VMEM((rows, units), F32),
            pltpu.VMEM((rows, units), BF16),
            pltpu.VMEM((n_dp, n_y, tok, fs), BF16),
            pltpu.VMEM((n_dp, n_y, tok, fs), BF16),
            pltpu.VMEM((n_dp, tok, fs), BF16),
            pltpu.VMEM((tok, pad_width), BF16),
            pltpu.VMEM((n_dp, tok, pad_width), BF16),
            dma((4,)),
            dma((n_dp, n_ep)),
            dma((n_dp,)),
            dma((n_dp, n_y)),
            dma((n_dp, n_y)),
            dma((n_dp, n_y)),
            dma((n_dp, n_y)),
            dma((n_dp, n_y)),
            dma((n_dp, n_y)),
            dma((n_dp,)),
            dma((n_dp,)),
            dma((n_dp,)),
            dma((n_dp,)),
        ],
        compiler_params=pltpu.CompilerParams(
            collective_id=0, has_side_effects=True, vmem_limit_bytes=60 * 2**20
        ),
    )(
        hidden_states,
        input_gain[None, :],
        expert_ids,
        route_scores,
        w_gate,
        w_up,
        w_down,
        latent_gain[None, :],
        w_latent,
        kv_gain[None, :],
        seq_lengths,
        seq_owners,
    )


def solution(mesh):
    return jax.shard_map(
        on_device,
        mesh=mesh,
        in_specs=(
            P(("grp", "ep"), "dp"),
            P("dp"),
            P(("grp", "ep"), None),
            P(("grp", "ep"), None),
            P("ep", None, "dp"),
            P("ep", None, "dp"),
            P("ep", "dp", None),
            P("dp"),
            P("dp", None),
            P(),
            P(("grp", "ep"), None),
            P(("grp", "ep"), None),
        ),
        out_specs=(P(("grp", "ep"), "dp"), P(("grp", "ep"), "dp", None, None)),
        check_vma=False,
    )
```

time: 296 us -> 91.2 us (0.31)
  waiting for transfers between devices: 180 us -> 0 us
  Pallas kernels: 0 us -> 77.5 us
  blocking collectives: 40.5 us -> 0 us
  matrix products: 20.6 us -> 0 us
  local copies, waits for them, and re-layouts: 30.3 us -> 12.6 us
  between operations: 14 us -> 0.64 us
  other arithmetic: 5.99 us -> 0 us
  starting transfers between devices: 4.03 us -> 0 us
    pallas_call x0 -> x1, Pallas kernels: none -> 77.5 us  [on_device(): pl.pallas_call(functools.partial(kernel, n_ep, n_dp), out_shape=(jax.Shap...]
    all_gather x1 -> x0, waiting for transfers between devices: 69.3 us -> none  [on_device(): feature_piece = lax.all_gather(arrived, 'dp', axis=2, tiled=True)]
    reduce_scatter x1 -> x0, waiting for transfers between devices: 66.3 us -> none  [on_device(): lax.psum_scatter(partial_value.astype(jnp.bfloat16), 'dp', scatter_dimens...]
    psum x1 -> x0, waiting for transfers between devices: 31.9 us -> none  [on_device(): lax.psum(latent_part.astype(jnp.bfloat16), 'dp').astype(jnp.float32)]
    psum x2 -> x0, blocking collectives: 24.3 us -> none  [the longest x1 13.5 us: on_device(): square_sum = lax.psum(jnp.sum(states * states, axis=1), 'dp')]
    dot_general x4 -> x0, matrix products: 20.6 us -> none  [the longest x1 12.1 us: on_device(): jnp.dot(hidden_units, down_matrix, preferred_element_type=jnp.float32)]
    all_to_all x1 -> x0, blocking collectives: 16.2 us -> none  [on_device(): lax.all_to_all(send_rows, 'ep', split_axis=1, concat_axis=1, tiled=True)]
    reshape x8 -> x0, local copies, waits for them, and re-layouts: 13.9 us -> none  [the longest x1 6.74 us: on_device(): piece_rows = feature_piece.reshape(row_count, piece_width)]
  transfers between devices with their start and end apart: 4 -> 0, of which waited for: 4 -> 0; matrix products, arithmetic and copies ran while one was open for 0% -> 0% of each run, Pallas kernels for 0% -> 0%
where the time goes in v1:
time: 91.2 us; the launch traced here: 90.8 us
  Pallas kernels  77.5 us (85%)
  local copies, waits for them, and re-layouts  12.6 us (14%)
    pallas_call x1, Pallas kernels, on_device(): pl.pallas_call(functools.partial(kernel, n_ep, n_dp), out_shape=(jax.Shap...  77.5 us
    unnamed x5, local copies, waits for them, and re-layouts  10 us

profile of v1, /device:TPU:0, one launch (start us, length us, event | category | flops | bytes accessed | tf_op | source)
XLA Modules:
  0.0 90.8 jit_solution(2238425865192025163)
XLA Ops:
  0.6 1.3 %broadcast_in_dim.9.gain_ref = f32[1,1792]{1,0:T(1,128)} reshape(f32[1792]{0:T(1024)} %param.13) | data formatting | bytes 14336 | tf_op jit(solution)/shard_map/broadcast_in_dim | solution.py:456
  1.9 1.3 %broadcast_in_dim.10.lgain_ref = f32[1,1792]{1,0:T(1,128)} reshape(f32[1792]{0:T(1024)} %param.19) | data formatting | bytes 14336 | tf_op jit(solution)/shard_map/broadcast_in_dim | solution.py:462
  3.2 1.4 %copy.14.ids_ref = s32[64,2]{1,0:T(8,128)} copy(s32[64,2]{0,1:T(2,128)} %param.14) | data formatting | bytes 1024 | tf_op args[2]
  4.6 1.4 %copy.15.scores_ref = f32[64,2]{1,0:T(8,128)} copy(f32[64,2]{0,1:T(2,128)} %param.15) | data formatting | bytes 1024 | tf_op args[3]
  6.0 4.1 %copy.16.wl_hbm = bf16[1792,576]{1,0:T(8,128)(2,1)} copy(bf16[1792,576]{0,1:T(8,128)(2,1)} %param.20) | data formatting | bytes 4128768 | tf_op args[8]
  10.1 77.5 %shard_map.131 = (bf16[64,1792]{1,0:T(8,128)(2,1)}, bf16[1,1,64,576]{3,2,1,0:T(8,128)(2,1)}) custom-call(bf16[64,1792]{1,0:T(8,128)(2,1)} %states_ref.1, f32[1,1792]{1,0:T(1,128)} %broadcast_in_dim.9.gain_ref, s32[64,2]{1,0:T(8,128)} %copy.14.ids_ref, f32[64,2]{1,0:T(8,128)} %copy.15.scores_ref, bf16[1,7168,512]{2,1,0:T(8,128)(2,1)} %wg_hbm.1, ...), custom_call_target="tpu_custom_call" | custom-call | tf_op jit(solution)/shard_map/pallas_call | solution.py:415
  87.6 1.6 %copy.19 = bf16[64,1792]{1,0:T(8,128)(2,1)} copy(bf16[64,1792]{1,0:T(8,128)(2,1)} %get-tuple-element.4) | data formatting | bytes 458752
  89.2 1.5 %copy.20 = bf16[1,1,64,576]{3,2,1,0:T(8,128)(2,1)} copy(bf16[1,1,64,576]{3,2,1,0:T(8,128)(2,1)} %get-tuple-element.5) | data formatting | bytes 147456

commit v2 on v1

--- a/solution.py
+++ b/solution.py
@@ -11,6 +11,7 @@
 EPSILON = 1e-06
 ROUTE_SCALE = 2.5
 LANES = 128
+PARTS = 2
 F32 = jnp.float32
 BF16 = jnp.bfloat16
 
@@ -82,18 +83,19 @@
     l_recv,
 ):
     tok, fs = states_ref.shape
-    top = ids_ref.shape[1]
+    top = ids_ref.shape[0]
     rows = n_ep * tok
     width = fs * n_dp
     n_y = n_ep // 2
     seqs = lengths_ref.shape[1]
-    kvl = kvgain_ref.shape[1]
-    lat_width = wl.shape[1]
+    kvl = kvgain_ref.shape[0]
+    lat_width = wl.shape[0]
     me = lax.axis_index("ep")
     z = lax.axis_index("dp")
     y = me // 2
     c = me % 2
     peer = y * 2 + (1 - c)
+    part = tok // PARTS
 
     def rem(src, dst, send, recv, **where):
         return pltpu.make_async_remote_copy(
@@ -128,52 +130,110 @@
     )
 
     states = states_ref[...].astype(F32)
-    xbuf[z, me, :, pl.ds(0, fs)] = (states * gain_ref[...]).astype(BF16)
+    xbuf[z, me, :, pl.ds(0, fs)] = (states * gain_ref[...][None, :]).astype(BF16)
     square = jnp.sum(states * states, axis=1, keepdims=True)
     scores = scores_ref[...]
-    weights = ROUTE_SCALE * scores / jnp.sum(scores, axis=1, keepdims=True)
+    weights = ROUTE_SCALE * scores / jnp.sum(scores, axis=0, keepdims=True)
+    half = LANES // 2
+    across = lax.broadcasted_iota(jnp.int32, (LANES, tok), 0) % half
+    named = jnp.zeros((LANES, tok), F32)
+    for k in range(top):
+        named += jnp.where(across == ids_ref[k : k + 1, :], weights[k : k + 1, :], 0.0)
     lane = lax.broadcasted_iota(jnp.int32, (tok, LANES), 1)
-    half = LANES // 2
-    folded = lane % half
-    extra = jnp.where(folded == n_ep, square, 0.0)
-    for k in range(top):
-        extra += jnp.where(folded == ids_ref[:, k : k + 1], weights[:, k : k + 1], 0.0)
+    extra = jnp.where(lane % half == n_ep, square, named.T)
     high, low = split_f32(extra)
     xbuf[z, me, :, pl.ds(fs, LANES)] = jnp.where(lane < half, high, low).astype(BF16)
 
     pl.semaphore_wait(barrier, n_dp - 1 + n_y - 1 + 1)
 
-    def gather_z(k):
-        to = flipped(z, k, n_dp)
-        return rem(xbuf.at[z, me], xbuf.at[z, me], gz_send.at[k], g_recv.at[z, me], dp=to)
-
-    def gather_y(s, j):
+    def block(s, b, h):
+        return xbuf.at[s, b, pl.ds(pl.multiple_of(h * part, part), part)]
+
+    def gather_z(s, h, way):
+        return rem(
+            block(s, me, h), block(s, me, h), gz_send.at[s, h, way], g_recv.at[s, me, h],
+            dp=(z + 2 * way - 1 + n_dp) % n_dp,
+        )
+
+    def relay(s, h, act):
+        @pl.when((s <= z) & (z + 1 < n_dp))
+        def _():
+            act(gather_z(s, h, 1))
+
+        @pl.when((s >= z) & (z > 0))
+        def _():
+            act(gather_z(s, h, 0))
+
+    def gather_y(s, j, h):
         to = ((y + j) % n_y) * 2 + c
-        return rem(xbuf.at[s, me], xbuf.at[s, me], gy_send.at[s, j], g_recv.at[s, me], ep=to)
-
-    def gather_c(s, yy):
+        return rem(
+            block(s, me, h), block(s, me, h), gy_send.at[s, j, h], g_recv.at[s, me, h], ep=to
+        )
+
+    def gather_c(s, yy, h):
         b = yy * 2 + c
-        return rem(xbuf.at[s, b], xbuf.at[s, b], gc_send.at[s, yy], g_recv.at[s, b], ep=peer)
-
-    def gather_wait(s, b):
-        rem(xbuf.at[s, b], xbuf.at[s, b], g_recv.at[s, b], g_recv.at[s, b], ep=peer).wait_recv()
-
-    loop(1, n_dp, lambda k: gather_z(k).start())
+        return rem(
+            block(s, b, h), block(s, b, h), gc_send.at[s, yy, h], g_recv.at[s, b, h], ep=peer
+        )
+
+    def gather_wait(s, b, h):
+        rem(
+            block(s, b, h), block(s, b, h), g_recv.at[s, b, h], g_recv.at[s, b, h], ep=peer
+        ).wait_recv()
+
+    def at_distance(i, body):
+        @pl.when(z - i >= 0)
+        def _():
+            body(z - i)
+
+        @pl.when((i > 0) & (z + i < n_dp))
+        def _():
+            body(z + i)
 
     acc_g[...] = jnp.zeros_like(acc_g)
     acc_u[...] = jnp.zeros_like(acc_u)
 
+    def spread(i):
+        def body(s):
+            def send(h):
+                @pl.when(i > 0)
+                def _():
+                    gather_wait(s, me, h)
+
+                relay(s, h, lambda copy: copy.start())
+                loop(1, n_y, lambda j: gather_y(s, j, h).start())
+                gather_c(s, y, h).start()
+
+            loop(0, PARTS, send)
+
+        at_distance(i, body)
+
+    def across_core(s):
+        def forward(j):
+            yy = (y + j) % n_y
+
+            def send(h):
+                gather_wait(s, yy * 2 + c, h)
+                gather_c(s, yy, h).start()
+
+            loop(0, PARTS, send)
+
+        loop(1, n_y, forward)
+
+    def multiply(s):
+        def arrive(yy):
+            loop(0, PARTS, lambda h: gather_wait(s, yy * 2 + (1 - c), h))
+
+        loop(0, n_y, arrive)
+        slab = xbuf[s, :, :, pl.ds(0, fs)].reshape(rows, fs)
+        depth = pl.ds(pl.multiple_of(s * fs, LANES), fs)
+        acc_g[...] += jnp.dot(slab, wg[depth, :], preferred_element_type=F32)
+        acc_u[...] += jnp.dot(slab, wu[depth, :], preferred_element_type=F32)
+
     def gather_step(i):
         @pl.when(i < n_dp)
         def _():
-            s = flipped(z, i, n_dp)
-
-            @pl.when(i > 0)
-            def _():
-                gather_wait(s, me)
-
-            loop(1, n_y, lambda j: gather_y(s, j).start())
-            gather_c(s, y).start()
+            spread(i)
 
         @pl.when(i == 0)
         def _():
@@ -182,14 +242,7 @@
 
         @pl.when((i >= 1) & (i <= n_dp))
         def _():
-            s = flipped(z, i - 1, n_dp)
-
-            def forward(j):
-                yy = (y + j) % n_y
-                gather_wait(s, yy * 2 + c)
-                gather_c(s, yy).start()
-
-            loop(1, n_y, forward)
+            at_distance(i - 1, across_core)
 
         @pl.when(i == 2)
         def _():
@@ -198,120 +251,158 @@
 
         @pl.when(i >= 2)
         def _():
-            s = flipped(z, i - 2, n_dp)
-            loop(0, n_y, lambda yy: gather_wait(s, yy * 2 + (1 - c)))
-            slab = xbuf[s, :, :, pl.ds(0, fs)].reshape(rows, fs)
-            depth = pl.ds(pl.multiple_of(s * fs, LANES), fs)
-            acc_g[...] += jnp.dot(slab, wg[depth, :], preferred_element_type=F32)
-            acc_u[...] += jnp.dot(slab, wu[depth, :], preferred_element_type=F32)
+            at_distance(i - 2, multiply)
 
     loop(0, n_dp + 2, gather_step)
 
     side = jnp.zeros((rows, LANES), F32)
     wide_lane = lax.broadcasted_iota(jnp.int32, (rows, LANES), 1) % half
     for s in range(n_dp):
-        part = xbuf[s, :, :, pl.ds(fs, LANES)].reshape(rows, LANES).astype(F32)
+        lanes = xbuf[s, :, :, pl.ds(fs, LANES)].reshape(rows, LANES).astype(F32)
         if s == 0:
-            route = jnp.sum(jnp.where(wide_lane == me, part, 0.0), axis=1, keepdims=True)
-        side += part
+            route = jnp.sum(jnp.where(wide_lane == me, lanes, 0.0), axis=1, keepdims=True)
+        side += lanes
     total = jnp.sum(jnp.where(wide_lane == n_ep, side, 0.0), axis=1, keepdims=True)
     scale = lax.rsqrt(total / width + EPSILON)
     gate = acc_g[...] * scale
     up = acc_u[...] * scale
     hid[...] = (route * (gate / (1.0 + jnp.exp(-gate)) * up)).astype(BF16)
 
-    loop(1, n_dp, lambda k: gather_z(k).wait_send())
-
     def gather_drain(s):
-        loop(1, n_y, lambda j: gather_y(s, j).wait_send())
-        loop(0, n_y, lambda yy: gather_c(s, yy).wait_send())
+        def drain(h):
+            relay(s, h, lambda copy: copy.wait_send())
+            loop(1, n_y, lambda j: gather_y(s, j, h).wait_send())
+            loop(0, n_y, lambda yy: gather_c(s, yy, h).wait_send())
+
+        loop(0, PARTS, drain)
 
     loop(0, n_dp, gather_drain)
     weight_copies[2].wait()
 
-    def slot(s, b):
-        return xbuf.at[s, b, :, pl.ds(0, fs)]
-
-    def reduce_c(s, yy):
-        return rem(
-            slot(s, yy * 2 + (1 - c)), crecv.at[s, yy], rc_send.at[s, yy], rc_recv.at[s, yy],
-            ep=peer,
-        )
-
-    def reduce_y(s, j):
+    def slot(s, b, h):
+        return xbuf.at[s, b, pl.ds(pl.multiple_of(h * part, part), part), pl.ds(0, fs)]
+
+    def half_of(buf, s, j, h):
+        return buf.at[s, j, pl.ds(pl.multiple_of(h * part, part), part)]
+
+    def reduce_c(s, yy, h):
+        return rem(
+            slot(s, yy * 2 + (1 - c), h), half_of(crecv, s, yy, h),
+            rc_send.at[s, yy, h], rc_recv.at[s, yy, h], ep=peer,
+        )
+
+    def reduce_y(s, j, h):
         to = (y + j) % n_y
         return rem(
-            slot(s, to * 2 + c), yrecv.at[s, j], ry_send.at[s, j], ry_recv.at[s, j],
-            ep=to * 2 + c,
-        )
-
-    def reduce_z(k):
-        to = flipped(z, k, n_dp)
-        return rem(slot(to, me), zrecv.at[k], rz_send.at[k], rz_recv.at[k], dp=to)
+            slot(s, to * 2 + c, h), half_of(yrecv, s, j, h),
+            ry_send.at[s, j, h], ry_recv.at[s, j, h], ep=to * 2 + c,
+        )
+
+    def reduce_z(s, h, way):
+        return rem(
+            slot(s, me, h), half_of(zrecv, way, s, h),
+            rz_send.at[s, h], rz_recv.at[way, s, h], dp=(z + 2 * way - 1 + n_dp) % n_dp,
+        )
+
+    def add_into(s, b, h, arrived):
+        here = slot(s, b, h)
+        here[...] = (here[...].astype(F32) + arrived[...].astype(F32)).astype(BF16)
+
+    def order(q):
+        ahead = n_dp - 1 - z
+        low = jnp.where(q < ahead, n_dp - 1 - q, q - ahead)
+        high = jnp.where(q < z, q, n_dp - 1 - (q - z))
+        return jnp.where(q == n_dp - 1, z, jnp.where(2 * z < n_dp, low, high))
 
     tile = 256 if fs % 256 == 0 else LANES
 
-    def reduce_step(i):
+    def produce_step(i):
         @pl.when(i < n_dp)
         def _():
-            s = flipped(z, n_dp - 1 - i, n_dp)
+            s = order(i)
             for n in range(fs // tile):
                 cols = pl.ds(pl.multiple_of(s * fs + n * tile, LANES), tile)
                 out = jnp.dot(hid[...], wd[:, cols], preferred_element_type=F32)
                 xbuf[s, :, :, pl.ds(n * tile, tile)] = out.astype(BF16).reshape(n_ep, tok, tile)
-            loop(1, n_y + 1, lambda j: reduce_c(s, (y + j) % n_y).start())
-
-        @pl.when((i >= 1) & (i <= n_dp))
-        def _():
-            s = flipped(z, n_dp - i, n_dp)
+
+            def send(j):
+                loop(0, PARTS, lambda h: reduce_c(s, (y + j) % n_y, h).start())
+
+            loop(1, n_y + 1, send)
+
+        @pl.when(i >= 1)
+        def _():
+            s = order(i - 1)
 
             def add(j):
                 yy = (y + j) % n_y
-                b = yy * 2 + c
-                reduce_c(s, yy).wait_recv()
-                xbuf[s, b, :, pl.ds(0, fs)] = (
-                    xbuf[s, b, :, pl.ds(0, fs)].astype(F32) + crecv[s, yy].astype(F32)
-                ).astype(BF16)
-
-                @pl.when(j < n_y)
+
+                def one(h):
+                    reduce_c(s, yy, h).wait_recv()
+                    add_into(s, yy * 2 + c, h, half_of(crecv, s, yy, h))
+
+                    @pl.when(j < n_y)
+                    def _():
+                        reduce_y(s, j, h).start()
+
+                loop(0, PARTS, one)
+
+            loop(1, n_y + 1, add)
+
+    loop(0, n_dp + 1, produce_step)
+
+    def reduce_step(i):
+        @pl.when(i < n_dp)
+        def _():
+            s = order(i)
+
+            def add(j):
+                def one(h):
+                    reduce_y(s, j, h).wait_recv()
+                    add_into(s, me, h, half_of(yrecv, s, j, h))
+
+                loop(0, PARTS, one)
+
+            loop(1, n_y, add)
+
+        @pl.when(i >= 1)
+        def _():
+            s = order(i - 1)
+
+            def one(h):
+                @pl.when((s >= z) & (z > 0))
                 def _():
-                    reduce_y(s, j).start()
-
-            loop(1, n_y + 1, add)
-
-        @pl.when(i >= 2)
-        def _():
-            k = n_dp + 1 - i
-            s = flipped(z, k, n_dp)
-
-            def add(j):
-                reduce_y(s, j).wait_recv()
-                xbuf[s, me, :, pl.ds(0, fs)] = (
-                    xbuf[s, me, :, pl.ds(0, fs)].astype(F32) + yrecv[s, j].astype(F32)
-                ).astype(BF16)
-
-            loop(1, n_y, add)
-
-            @pl.when(k > 0)
-            def _():
-                reduce_z(k).start()
-
-    loop(0, n_dp + 2, reduce_step)
+                    reduce_z(s, h, 1).wait_recv()
+                    add_into(s, me, h, half_of(zrecv, 1, s, h))
+
+                @pl.when((s <= z) & (z < n_dp - 1))
+                def _():
+                    reduce_z(s, h, 0).wait_recv()
+                    add_into(s, me, h, half_of(zrecv, 0, s, h))
+
+                @pl.when(s > z)
+                def _():
+                    reduce_z(s, h, 1).start()
+
+                @pl.when(s < z)
+                def _():
+                    reduce_z(s, h, 0).start()
+
+            loop(0, PARTS, one)
+
+    loop(0, n_dp + 1, reduce_step)
 
     routed = xbuf[z, me, :, pl.ds(0, fs)].astype(F32)
-    for k in range(n_dp - 1, 0, -1):
-        reduce_z(k).wait_recv()
-        routed += zrecv[k].astype(F32)
     mixed = (states_ref[...].astype(F32) + routed).astype(BF16)
     mixed_ref[...] = mixed
 
     layer = mixed.astype(F32)
-    gained = (layer * lgain_ref[...]).astype(BF16)
+    gained = (layer * lgain_ref[...][None, :]).astype(BF16)
     out_square = jnp.sum(layer * layer, axis=1, keepdims=True)
     weight_copies[3].wait()
     pad_width = latbuf.shape[1]
-    latbuf[:, pl.ds(0, lat_width)] = jnp.dot(
-        gained, wl[...], preferred_element_type=F32
+    latbuf[:, pl.ds(0, lat_width)] = lax.dot_general(
+        gained, wl[...], (((1,), (1,)), ((), ())), preferred_element_type=F32
     ).astype(BF16)
     high, low = split_f32(out_square)
     spare = lax.broadcasted_iota(jnp.int32, (tok, pad_width - lat_width), 1)
@@ -362,7 +453,7 @@
     out_scale = lax.rsqrt(jnp.sum(in_square, axis=1, keepdims=True) / width + EPSILON)
     compressed = summed[:, :kvl] * out_scale
     mean_square = jnp.mean(compressed * compressed, axis=1, keepdims=True)
-    normed = compressed * lax.rsqrt(mean_square + EPSILON) * kvgain_ref[...]
+    normed = compressed * lax.rsqrt(mean_square + EPSILON) * kvgain_ref[...][None, :]
     keys = end_part * out_scale
     swapped = jnp.where(
         column < turn, pltpu.roll(keys, tail - turn, 1), pltpu.roll(keys, turn, 1)
@@ -376,11 +467,17 @@
 
     for k in range(1, n_dp):
         latent(k).wait_send()
-        reduce_z(k).wait_send()
 
     def reduce_drain(s):
-        loop(1, n_y, lambda j: reduce_y(s, j).wait_send())
-        loop(0, n_y, lambda yy: reduce_c(s, yy).wait_send())
+        def drain(h):
+            @pl.when(s != z)
+            def _():
+                reduce_z(s, h, 1).wait_send()
+
+            loop(1, n_y, lambda j: reduce_y(s, j, h).wait_send())
+            loop(0, n_y, lambda yy: reduce_c(s, yy, h).wait_send())
+
+        loop(0, PARTS, drain)
 
     loop(0, n_dp, reduce_drain)
 
@@ -425,26 +522,26 @@
             pltpu.VMEM((width, units), BF16),
             pltpu.VMEM((width, units), BF16),
             pltpu.VMEM((units, width), BF16),
-            pltpu.VMEM((fs, lat_width), BF16),
+            pltpu.VMEM((lat_width, fs), BF16),
             pltpu.VMEM((rows, units), F32),
             pltpu.VMEM((rows, units), F32),
             pltpu.VMEM((rows, units), BF16),
             pltpu.VMEM((n_dp, n_y, tok, fs), BF16),
             pltpu.VMEM((n_dp, n_y, tok, fs), BF16),
-            pltpu.VMEM((n_dp, tok, fs), BF16),
+            pltpu.VMEM((2, n_dp, tok, fs), BF16),
             pltpu.VMEM((tok, pad_width), BF16),
             pltpu.VMEM((n_dp, tok, pad_width), BF16),
             dma((4,)),
-            dma((n_dp, n_ep)),
-            dma((n_dp,)),
-            dma((n_dp, n_y)),
-            dma((n_dp, n_y)),
-            dma((n_dp, n_y)),
-            dma((n_dp, n_y)),
-            dma((n_dp, n_y)),
-            dma((n_dp, n_y)),
-            dma((n_dp,)),
-            dma((n_dp,)),
+            dma((n_dp, n_ep, PARTS)),
+            dma((n_dp, PARTS, 2)),
+            dma((n_dp, n_y, PARTS)),
+            dma((n_dp, n_y, PARTS)),
+            dma((n_dp, n_y, PARTS)),
+            dma((n_dp, n_y, PARTS)),
+            dma((n_dp, n_y, PARTS)),
+            dma((n_dp, n_y, PARTS)),
+            dma((n_dp, PARTS)),
+            dma((2, n_dp, PARTS)),
             dma((n_dp,)),
             dma((n_dp,)),
         ],
@@ -453,15 +550,15 @@
         ),
     )(
         hidden_states,
-        input_gain[None, :],
-        expert_ids,
-        route_scores,
+        input_gain,
+        expert_ids.T,
+        route_scores.T,
         w_gate,
         w_up,
         w_down,
-        latent_gain[None, :],
-        w_latent,
-        kv_gain[None, :],
+        latent_gain,
+        w_latent.T,
+        kv_gain,
         seq_lengths,
         seq_owners,
     )

time: 91.2 us -> 77 us (0.84)
  local copies, waits for them, and re-layouts: 12.6 us -> 3.17 us
  Pallas kernels: 77.5 us -> 73 us
    unnamed x5 -> x2, local copies, waits for them, and re-layouts: 10 us -> 3.17 us
    pallas_call x1, Pallas kernels: 77.5 us -> 73 us  [on_device(): pl.pallas_call(functools.partial(kernel, n_ep, n_dp), out_shape=(jax.Shap...]
    broadcast_in_dim x2 -> x0, local copies, waits for them, and re-layouts: 2.59 us -> none  [the longest x1 1.3 us: on_device(): input_gain[None, :]]
where the time goes in v2:
time: 77 us; the launch traced here: 76.8 us
  Pallas kernels  73 us (95%)
  local copies, waits for them, and re-layouts  3.17 us (4%)
    pallas_call x1, Pallas kernels, on_device(): pl.pallas_call(functools.partial(kernel, n_ep, n_dp), out_shape=(jax.Shap...  73 us
    unnamed x2, local copies, waits for them, and re-layouts  3.17 us

profile of v2, /device:TPU:0, one launch (start us, length us, event | category | flops | bytes accessed | tf_op | source)
XLA Modules:
  0.0 76.8 jit_solution(11794363779579450594)
XLA Ops:
  0.6 73.0 %shard_map.131 = (bf16[64,1792]{1,0:T(8,128)(2,1)}, bf16[1,1,64,576]{3,2,1,0:T(8,128)(2,1)}) custom-call(bf16[64,1792]{1,0:T(8,128)(2,1)} %states_ref.1, f32[1792]{0:T(1024)} %gain_ref.1, s32[2,64]{1,0:T(2,128)} %bitcast.4, f32[2,64]{1,0:T(2,128)} %bitcast.5, bf16[1,7168,512]{2,1,0:T(8,128)(2,1)} %wg_hbm.1, bf16[1,7168,512]{2,1,0:T(8,128)(2,1)} %wu_hbm.1, ...), custom_call_target="tpu_custom_call" | custom-call | tf_op jit(solution)/shard_map/pallas_call | solution.py:512
  73.6 1.6 %copy.16 = bf16[64,1792]{1,0:T(8,128)(2,1)} copy(bf16[64,1792]{1,0:T(8,128)(2,1)} %get-tuple-element.4) | data formatting | bytes 458752
  75.3 1.5 %copy.17 = bf16[1,1,64,576]{3,2,1,0:T(8,128)(2,1)} copy(bf16[1,1,64,576]{3,2,1,0:T(8,128)(2,1)} %get-tuple-element.5) | data formatting | bytes 147456

commit v3 on v2

--- a/solution.py
+++ b/solution.py
@@ -240,10 +240,6 @@
             for copy in weight_copies:
                 copy.start()
 
-        @pl.when((i >= 1) & (i <= n_dp))
-        def _():
-            at_distance(i - 1, across_core)
-
         @pl.when(i == 2)
         def _():
             weight_copies[0].wait()
@@ -252,6 +248,10 @@
         @pl.when(i >= 2)
         def _():
             at_distance(i - 2, multiply)
+
+        @pl.when((i >= 1) & (i <= n_dp))
+        def _():
+            at_distance(i - 1, across_core)
 
     loop(0, n_dp + 2, gather_step)
 

time: 77 us -> 75.4 us (0.979)
  Pallas kernels: 73 us -> 71.4 us
    pallas_call x1, Pallas kernels: 73 us -> 71.4 us  [on_device(): pl.pallas_call(functools.partial(kernel, n_ep, n_dp), out_shape=(jax.Shap...]
where the time goes in v3:
time: 75.4 us; the launch traced here: 75.2 us
  Pallas kernels  71.4 us (95%)
  local copies, waits for them, and re-layouts  3.17 us (4%)
    pallas_call x1, Pallas kernels, on_device(): pl.pallas_call(functools.partial(kernel, n_ep, n_dp), out_shape=(jax.Shap...  71.4 us
    unnamed x2, local copies, waits for them, and re-layouts  3.17 us

profile of v3, /device:TPU:0, one launch (start us, length us, event | category | flops | bytes accessed | tf_op | source)
XLA Modules:
  0.0 75.2 jit_solution(8133563092977380410)
XLA Ops:
  0.6 71.4 %shard_map.131 = (bf16[64,1792]{1,0:T(8,128)(2,1)}, bf16[1,1,64,576]{3,2,1,0:T(8,128)(2,1)}) custom-call(bf16[64,1792]{1,0:T(8,128)(2,1)} %states_ref.1, f32[1792]{0:T(1024)} %gain_ref.1, s32[2,64]{1,0:T(2,128)} %bitcast.4, f32[2,64]{1,0:T(2,128)} %bitcast.5, bf16[1,7168,512]{2,1,0:T(8,128)(2,1)} %wg_hbm.1, bf16[1,7168,512]{2,1,0:T(8,128)(2,1)} %wu_hbm.1, ...), custom_call_target="tpu_custom_call" | custom-call | tf_op jit(solution)/shard_map/pallas_call | solution.py:512
  72.1 1.6 %copy.16 = bf16[64,1792]{1,0:T(8,128)(2,1)} copy(bf16[64,1792]{1,0:T(8,128)(2,1)} %get-tuple-element.4) | data formatting | bytes 458752
  73.7 1.5 %copy.17 = bf16[1,1,64,576]{3,2,1,0:T(8,128)(2,1)} copy(bf16[1,1,64,576]{3,2,1,0:T(8,128)(2,1)} %get-tuple-element.5) | data formatting | bytes 147456
